TPU v7x, 32 devices: a whole 2x2x4 slice. The times are simulated.
32 devices in a mesh: dp: 16 (over z, y, core), book: 2 (over x).
Axes of the slice: x: 2, y: 2, z: 4, core: 2. Of those that a mesh axis runs over, the one named last changes fastest.
Arguments:
- corpus_rows: bfloat16 [12288, 1024], P('dp'), may hold values from -6 to 6
- code_ids: int32 [12288, 8], P('dp', 'book'), may hold values from 0 to 2047
- master: float32 [8, 2048, 1024], P('book', 'dp'), may hold values from -5 to 5
- first_moment: float32 [8, 2048, 1024], P('book', 'dp'), may hold values from -6 to 6
- second_moment: float32 [8, 2048, 1024], P('book', 'dp'), may hold values from 1 to 30
Outputs:
- new_master: float32 [8, 2048, 1024], P('book', 'dp')
- new_first: float32 [8, 2048, 1024], P('book', 'dp')
- new_second: float32 [8, 2048, 1024], P('book', 'dp')
All inputs are finite; a program needn't handle non-finite values.
Results may differ from a plain program's by a relative error of at most 0.002.
Values may be sent and summed in bfloat16 or wider, within the bound.
A program may use at most 192 MiB of HBM per device.

v0:
```python
import jax
import jax.numpy as jnp
from jax import lax
from jax.sharding import PartitionSpec as P

STEPS = 2


def make_pull(corpus_rows, recon):
    values = corpus_rows.astype(jnp.float32)
    resid = values - recon
    unit = values * lax.rsqrt(jnp.sum(values * values, axis=-1, keepdims=True) + 1e-06)
    along = jnp.sum(resid * unit, axis=-1, keepdims=True)
    return (resid + 3.0 * along * unit).astype(jnp.bfloat16)


def per_device(corpus_rows, code_ids, master, first_moment, second_moment):
    book_count = master.shape[0]
    shard_rows = master.shape[1]
    width = master.shape[2]
    local_rows = corpus_rows.shape[0]
    for turn_index in range(STEPS):
        books = master.astype(jnp.bfloat16)
        empty = jnp.zeros((local_rows, width), jnp.float32)
        full_books = lax.all_gather(books, "dp", axis=1, tiled=True)
        partial_value = empty
        for book_slot in range(book_count):
            partial_value = partial_value + jnp.take(
                full_books[book_slot], code_ids[:, book_slot], axis=0
            ).astype(jnp.float32)
        recon = lax.psum(partial_value, "book")
        pull = make_pull(corpus_rows, recon)
        columns = lax.broadcasted_iota(jnp.int32, (1, lax.axis_size("dp") * shard_rows), 1)
        blocks = []
        for grad_book_slot in range(book_count):
            one_hot = (code_ids[:, grad_book_slot][:, None] == columns).astype(jnp.bfloat16)
            summed = lax.dot_general(
                one_hot, pull, (((0,), (0,)), ((), ())), preferred_element_type=jnp.float32
            )
            blocks.append(-2.0 * summed)
        grad_flat = lax.psum_scatter(
            jnp.concatenate(blocks, axis=1), "dp", scatter_dimension=0, tiled=True
        )
        grad = jnp.transpose(grad_flat.reshape(shard_rows, book_count, width), (1, 0, 2))
        first_moment = 0.9 * first_moment + 0.1 * grad
        second_moment = 0.99 * second_moment + 0.01 * grad * grad
        master = master - 0.05 * first_moment / (jnp.sqrt(second_moment) + 1e-08)
    return (master, first_moment, second_moment)


def solution(mesh):
    in_specs = (
        P("dp", None),
        P("dp", "book"),
        P("book", "dp", None),
        P("book", "dp", None),
        P("book", "dp", None),
    )
    out_specs = (P("book", "dp", None), P("book", "dp", None), P("book", "dp", None))
    return jax.shard_map(
        per_device, mesh=mesh, in_specs=in_specs, out_specs=out_specs, check_vma=False
    )
```

profile of v0, /device:TPU:0, one launch (start us, length us, event | category | flops | bytes accessed | tf_op | source)
XLA Modules:
  0.0 1295.0 jit_solution(10355159778973246720)
XLA Ops:
  7.2 0.0 copy-start.4
  7.2 0.0 all-gather.3.cloned.1.call-start
  7.2 2.7 convert_element_type.49
  9.9 0.0 all-gather.3.cloned.1.call-update
  10.0 0.0 all-reduce.3.cloned.1.call-start
  10.0 0.0 copy-done.4
  10.2 130.2 %all-gather.3.cloned.1.call-done = bf16[4,2048,1024]{2,1,0:T(8,128)(2,1)} async-done(((bf16[4,128,1024]{2,1,0:T(8,128)(2,1)}), bf16[4,2048,1024]{2,1,0:T(8,128)(2,1)}) %all-gather.3.cloned.1.call-update) | async-done | bytes 16777232 | tf_op jit(solution)/shard_map/all_gather | solution.py:25
  140.4 12.2 slice_bitcast_fusion.7
  152.6 6.5 gather_fusion
  159.2 6.5 gather_fusion.3
  165.7 7.3 gather_fusion.2
  173.0 7.3 gather_fusion.1
  180.3 4.0 convert_add_fusion.1
  184.3 0.0 copy-start
  184.3 0.0 all-reduce.3.cloned.1.call-update
  184.3 0.2 reduce-scatter.3.cloned.1.call-start
  184.6 1.2 copy-done
  185.7 0.4 fusion.26
  186.1 82.3 %all-reduce.3.cloned.1.call-done = f32[768,1024]{1,0:T(8,128)} async-done(((f32[768,1024]{1,0:T(8,128)}), f32[768,1024]{1,0:T(8,128)}) %all-reduce.3.cloned.1.call-update) | async-done | bytes 3145744 | tf_op jit(solution)/shard_map/psum | solution.py:31
  268.4 0.0 copy-start.2
  268.4 2.8 fusion.20
  271.2 0.0 copy-done.2
  271.2 0.7 fusion.22
  271.9 3.8 fusion.18
  275.7 3.8 fusion.16
  279.5 6.2 fusion.14
  285.7 6.0 fusion.12
  291.7 18.8 %pad_maximum_fusion = f32[2048,4096]{0,1:T(8,128)} fusion(f32[2048,1024]{0,1:T(8,128)S(1)} %fusion.18, f32[2048,1024]{0,1:T(8,128)S(1)} %fusion.16, f32[2048,1024]{0,1:T(8,128)} %fusion.14, f32[2048,1024]{0,1:T(8,128)} %fusion.12), kind=kLoop, calls=%fused_computation.8 | loop fusion | flops 25165824 | bytes 67108864 | tf_op jit(solution)/shard_map/concatenate | solution.py:42
  310.5 0.0 reduce-scatter.3.cloned.1.call-update
  310.6 0.0 all-gather.5.cloned.1.call-start
  310.6 332.9 %reduce-scatter.3.cloned.1.call-done = f32[128,4096]{0,1:T(8,128)} async-done(((f32[2048,4096]{0,1:T(8,128)}), f32[128,4096]{0,1:T(8,128)}) %reduce-scatter.3.cloned.1.call-update) | async-done | bytes 2097168 | tf_op jit(solution)/shard_map/reduce_scatter | solution.py:41
  643.5 2.9 copy.8
  646.4 6.5 fusion.41
  652.8 0.0 all-gather.5.cloned.1.call-update
  652.9 0.0 all-reduce.5.cloned.1.call-start
  652.9 126.0 %all-gather.5.cloned.1.call-done = bf16[4,2048,1024]{2,1,0:T(8,128)(2,1)} async-done(((bf16[4,128,1024]{2,1,0:T(8,128)(2,1)}), bf16[4,2048,1024]{2,1,0:T(8,128)(2,1)}) %all-gather.5.cloned.1.call-update) | async-done | bytes 16777232 | tf_op jit(solution)/shard_map/all_gather | solution.py:25
  778.9 12.6 slice_bitcast_fusion.3
  791.5 6.5 gather_fusion.4
  798.0 7.3 gather_fusion.7
  805.3 7.3 gather_fusion.6
  812.6 7.3 gather_fusion.5
  819.9 4.3 convert_add_fusion
  824.2 0.0 all-reduce.5.cloned.1.call-update
  824.2 0.2 reduce-scatter.5.cloned.1.call-start
  824.5 83.9 %all-reduce.5.cloned.1.call-done = f32[768,1024]{1,0:T(8,128)} async-done(((f32[768,1024]{1,0:T(8,128)}), f32[768,1024]{1,0:T(8,128)}) %all-reduce.5.cloned.1.call-update) | async-done | bytes 3145744 | tf_op jit(solution)/shard_map/psum | solution.py:31
  908.3 0.0 copy-start.3
  908.3 2.8 fusion.23
  911.1 0.0 copy-done.3
  911.2 0.7 fusion.25
  911.9 3.8 fusion.19
  915.6 3.8 fusion.17
  919.4 4.0 fusion.15
  923.4 6.0 fusion.13
  929.4 14.9 %pad_maximum_fusion.1 = f32[2048,4096]{0,1:T(8,128)} fusion(f32[2048,1024]{0,1:T(8,128)S(1)} %fusion.19, f32[2048,1024]{0,1:T(8,128)S(1)} %fusion.17, f32[2048,1024]{0,1:T(8,128)S(1)} %fusion.15, f32[2048,1024]{0,1:T(8,128)} %fusion.13), kind=kLoop, calls=%fused_computation.9 | loop fusion | flops 25165824 | bytes 67108864 | tf_op jit(solution)/shard_map/concatenate | solution.py:42
  944.3 0.0 reduce-scatter.5.cloned.1.call-update
  944.3 332.9 %reduce-scatter.5.cloned.1.call-done = f32[128,4096]{0,1:T(8,128)} async-done(((f32[2048,4096]{0,1:T(8,128)}), f32[128,4096]{0,1:T(8,128)}) %reduce-scatter.5.cloned.1.call-update) | async-done | bytes 2097168 | tf_op jit(solution)/shard_map/reduce_scatter | solution.py:41
  1277.2 0.0 copy-start.1
  1277.2 3.0 copy.9
  1280.3 0.0 copy-done.1
  1280.3 7.6 divide_subtract_fusion
  (12 shorter events, 0.1 us)
Async XLA Ops:
  7.2 2.9 copy-start.4
  7.2 133.3 %all-gather.3.cloned.1.call-start = ((), (), s32[]{:S(2)}) async-start(), calls=%async_computation.2 | async-start | bytes 17825792 | tf_op jit(solution)/shard_map/all_gather | solution.py:25
  10.0 258.4 %all-reduce.3.cloned.1.call-start = ((), (), s32[]{:S(2)}) async-start(), calls=%async_computation.3 | async-start | bytes 6291456 | tf_op jit(solution)/shard_map/psum | solution.py:31
  184.3 1.4 copy-start
  184.3 459.1 %reduce-scatter.3.cloned.1.call-start = ((), (), s32[]{:S(2)}) async-start(), calls=%async_computation.4 | async-start | bytes 35651584 | tf_op jit(solution)/shard_map/reduce_scatter | solution.py:41
  268.4 2.8 copy-start.2
  310.6 468.4 %all-gather.5.cloned.1.call-start = ((), (), s32[]{:S(2)}) async-start(), calls=%async_computation.5 | async-start | bytes 17825792 | tf_op jit(solution)/shard_map/all_gather | solution.py:25
  652.9 255.5 %all-reduce.5.cloned.1.call-start = ((), (), s32[]{:S(2)}) async-start(), calls=%async_computation.6 | async-start | bytes 6291456 | tf_op jit(solution)/shard_map/psum | solution.py:31
  824.2 453.0 %reduce-scatter.5.cloned.1.call-start = ((), (), s32[]{:S(2)}) async-start(), calls=%async_computation.7 | async-start | bytes 35651584 | tf_op jit(solution)/shard_map/reduce_scatter | solution.py:41
  908.3 2.8 copy-start.3
  1277.2 3.0 copy-start.1
Sparse Core Ops, SparseCore 0:
  10.8 129.6 all-gather.2
  184.5 83.9 all-reduce.2
  310.7 332.7 reduce-scatter.2
  653.0 125.9 all-gather.4
  824.4 83.9 all-reduce.4
  944.5 332.7 reduce-scatter.4
where the time goes:
time: 1300 us; the launch traced here: 1290 us
  waiting for transfers between devices  1090 us (84%)
  local copies, waits for them, and re-layouts  88 us (7%)
  other arithmetic  66.3 us (5%)
  matrix products  37.3 us (3%)
  between operations  14.5 us (1%)
    reduce_scatter x2, waiting for transfers between devices, per_device(): lax.psum_scatter(jnp.concatenate(blocks, axis=1), 'dp', scatter_dimension...  666 us
    all_gather x2, waiting for transfers between devices, per_device(): full_books = lax.all_gather(books, 'dp', axis=1, tiled=True)  256 us
    psum x2, waiting for transfers between devices, per_device(): recon = lax.psum(partial_value, 'book')  166 us
    gather x8, local copies, waits for them, and re-layouts, per_device(): jnp.take(full_books[book_slot], code_ids[:, book_slot], axis=0)  56 us
    dot_general x8, matrix products, per_device(): lax.dot_general(one_hot, pull, (((0,), (0,)), ((), ())), preferred_elemen...  37.3 us
    concatenate x2, other arithmetic, per_device(): jnp.concatenate(blocks, axis=1)  33.7 us
  transfers between devices with their start and end apart: 6, of which 6 were waited for; matrix products, arithmetic and copies ran while one was open for 0% of the time, Pallas kernels for 0%

commit v1 on v0

--- a/solution.py
+++ b/solution.py
@@ -28,7 +28,8 @@
             partial_value = partial_value + jnp.take(
                 full_books[book_slot], code_ids[:, book_slot], axis=0
             ).astype(jnp.float32)
-        recon = lax.psum(partial_value, "book")
+        parts = lax.all_gather(partial_value, "book")
+        recon = jnp.sum(parts, axis=0)
         pull = make_pull(corpus_rows, recon)
         columns = lax.broadcasted_iota(jnp.int32, (1, lax.axis_size("dp") * shard_rows), 1)
         blocks = []

time: 1300 us -> 1300 us (level)
    psum x2 -> x0, waiting for transfers between devices: 166 us -> none  [per_device(): recon = lax.psum(partial_value, 'book')]
    all_gather x0 -> x2, waiting for transfers between devices: none -> 155 us  [per_device(): parts = lax.all_gather(partial_value, 'book')]
where the time goes in v1:
time: 1300 us
  waiting for transfers between devices  1080 us (83%)
  local copies, waits for them, and re-layouts  88 us (7%)
  other arithmetic  77.3 us (6%)
  matrix products  37.3 us (3%)
  between operations  14.5 us (1%)
    reduce_scatter x2, waiting for transfers between devices, per_device(): lax.psum_scatter(jnp.concatenate(blocks, axis=1), 'dp', scatter_dimension...  666 us
    all_gather x2, waiting for transfers between devices, per_device(): full_books = lax.all_gather(books, 'dp', axis=1, tiled=True)  256 us
    all_gather x2, waiting for transfers between devices, per_device(): parts = lax.all_gather(partial_value, 'book')  155 us
    gather x8, local copies, waits for them, and re-layouts, per_device(): jnp.take(full_books[book_slot], code_ids[:, book_slot], axis=0)  56 us
    dot_general x8, matrix products, per_device(): lax.dot_general(one_hot, pull, (((0,), (0,)), ((), ())), preferred_elemen...  37.3 us
    concatenate x2, other arithmetic, per_device(): jnp.concatenate(blocks, axis=1)  33.7 us
  transfers between devices with their start and end apart: 6, of which 6 were waited for; matrix products, arithmetic and copies ran while one was open for 0% of the time, Pallas kernels for 0%

profile of v1, /device:TPU:0, one launch (start us, length us, event | category | flops | bytes accessed | tf_op | source)
XLA Modules:
  0.0 1295.3 jit_solution(6842992515241666089)
XLA Ops:
  7.2 0.0 copy-start.4
  7.2 0.0 all-gather.7.cloned.1.call-start
  7.2 2.7 convert_element_type.49
  9.9 0.0 all-gather.7.cloned.1.call-update
  10.0 0.0 all-gather.11.cloned.1.call-start
  10.0 0.0 copy-done.4
  10.2 130.2 %all-gather.7.cloned.1.call-done = bf16[4,2048,1024]{2,1,0:T(8,128)(2,1)} async-done(((bf16[4,128,1024]{2,1,0:T(8,128)(2,1)}), bf16[4,2048,1024]{2,1,0:T(8,128)(2,1)}) %all-gather.7.cloned.1.call-update) | async-done | bytes 16777232 | tf_op jit(solution)/shard_map/all_gather | solution.py:25
  140.4 12.2 slice_bitcast_fusion.7
  152.6 6.5 gather_fusion
  159.2 6.5 gather_fusion.3
  165.7 7.3 gather_fusion.2
  173.0 7.3 gather_fusion.1
  180.3 4.1 convert_add_fusion.1
  184.4 0.0 copy-start
  184.4 0.0 all-gather.11.cloned.1.call-update
  184.4 0.2 reduce-scatter.3.cloned.1.call-start
  184.6 1.2 copy-done
  185.8 0.4 fusion.26
  186.2 76.9 %all-gather.11.cloned.1.call-done = f32[1536,1024]{1,0:T(8,128)} async-done(((f32[768,1024]{1,0:T(8,128)}), f32[1536,1024]{1,0:T(8,128)}) %all-gather.11.cloned.1.call-update) | async-done | bytes 6291472 | tf_op jit(solution)/shard_map/all_gather | solution.py:31
  263.1 5.4 reduce_sum.49
  268.5 0.0 copy-start.2
  268.5 2.8 fusion.20
  271.3 0.0 copy-done.2
  271.4 0.7 fusion.22
  272.1 3.8 fusion.18
  275.8 3.8 fusion.16
  279.6 6.2 fusion.14
  285.9 6.0 fusion.12
  291.8 18.8 %pad_maximum_fusion = f32[2048,4096]{0,1:T(8,128)} fusion(f32[2048,1024]{0,1:T(8,128)S(1)} %fusion.18, f32[2048,1024]{0,1:T(8,128)S(1)} %fusion.16, f32[2048,1024]{0,1:T(8,128)} %fusion.14, f32[2048,1024]{0,1:T(8,128)} %fusion.12), kind=kLoop, calls=%fused_computation.8 | loop fusion | flops 25165824 | bytes 67108864 | tf_op jit(solution)/shard_map/concatenate | solution.py:43
  310.7 0.0 reduce-scatter.3.cloned.1.call-update
  310.7 0.0 all-gather.9.cloned.1.call-start
  310.7 332.8 %reduce-scatter.3.cloned.1.call-done = f32[128,4096]{0,1:T(8,128)} async-done(((f32[2048,4096]{0,1:T(8,128)}), f32[128,4096]{0,1:T(8,128)}) %reduce-scatter.3.cloned.1.call-update) | async-done | bytes 2097168 | tf_op jit(solution)/shard_map/reduce_scatter | solution.py:42
  643.6 2.9 copy.8
  646.4 6.5 fusion.41
  652.9 0.0 all-gather.9.cloned.1.call-update
  653.0 0.0 all-gather.13.cloned.1.call-start
  653.0 126.1 %all-gather.9.cloned.1.call-done = bf16[4,2048,1024]{2,1,0:T(8,128)(2,1)} async-done(((bf16[4,128,1024]{2,1,0:T(8,128)(2,1)}), bf16[4,2048,1024]{2,1,0:T(8,128)(2,1)}) %all-gather.9.cloned.1.call-update) | async-done | bytes 16777232 | tf_op jit(solution)/shard_map/all_gather | solution.py:25
  779.1 12.6 slice_bitcast_fusion.3
  791.7 6.5 gather_fusion.4
  798.2 7.3 gather_fusion.7
  805.5 7.3 gather_fusion.6
  812.8 7.3 gather_fusion.5
  820.1 4.4 convert_add_fusion
  824.5 0.0 all-gather.13.cloned.1.call-update
  824.5 0.2 reduce-scatter.5.cloned.1.call-start
  824.7 78.5 %all-gather.13.cloned.1.call-done = f32[1536,1024]{1,0:T(8,128)} async-done(((f32[768,1024]{1,0:T(8,128)}), f32[1536,1024]{1,0:T(8,128)}) %all-gather.13.cloned.1.call-update) | async-done | bytes 6291472 | tf_op jit(solution)/shard_map/all_gather | solution.py:31
  903.2 5.4 reduce_sum.52
  908.6 0.0 copy-start.1
  908.6 2.8 fusion.23
  911.4 0.0 copy-done.1
  911.5 0.7 fusion.25
  912.2 3.8 fusion.19
  915.9 3.8 fusion.17
  919.7 4.0 fusion.15
  923.7 6.0 fusion.13
  929.7 14.9 %pad_maximum_fusion.1 = f32[2048,4096]{0,1:T(8,128)} fusion(f32[2048,1024]{0,1:T(8,128)S(1)} %fusion.19, f32[2048,1024]{0,1:T(8,128)S(1)} %fusion.17, f32[2048,1024]{0,1:T(8,128)S(1)} %fusion.15, f32[2048,1024]{0,1:T(8,128)} %fusion.13), kind=kLoop, calls=%fused_computation.9 | loop fusion | flops 25165824 | bytes 67108864 | tf_op jit(solution)/shard_map/concatenate | solution.py:43
  944.6 0.0 reduce-scatter.5.cloned.1.call-update
  944.7 332.9 %reduce-scatter.5.cloned.1.call-done = f32[128,4096]{0,1:T(8,128)} async-done(((f32[2048,4096]{0,1:T(8,128)}), f32[128,4096]{0,1:T(8,128)}) %reduce-scatter.5.cloned.1.call-update) | async-done | bytes 2097168 | tf_op jit(solution)/shard_map/reduce_scatter | solution.py:42
  1277.6 0.0 copy-start.3
  1277.6 3.0 copy.9
  1280.6 0.0 copy-done.3
  1280.6 7.6 divide_subtract_fusion
  (12 shorter events, 0.1 us)
Async XLA Ops:
  7.2 2.9 copy-start.4
  7.2 133.3 %all-gather.7.cloned.1.call-start = ((), (), s32[]{:S(2)}) async-start(), calls=%async_computation.2 | async-start | bytes 17825792 | tf_op jit(solution)/shard_map/all_gather | solution.py:25
  10.0 253.1 %all-gather.11.cloned.1.call-start = ((), (), s32[]{:S(2)}) async-start(), calls=%async_computation.6 | async-start | bytes 9437184 | tf_op jit(solution)/shard_map/all_gather | solution.py:31
  184.4 1.4 copy-start
  184.4 459.2 %reduce-scatter.3.cloned.1.call-start = ((), (), s32[]{:S(2)}) async-start(), calls=%async_computation.3 | async-start | bytes 35651584 | tf_op jit(solution)/shard_map/reduce_scatter | solution.py:42
  268.5 2.8 copy-start.2
  310.7 468.4 %all-gather.9.cloned.1.call-start = ((), (), s32[]{:S(2)}) async-start(), calls=%async_computation.4 | async-start | bytes 17825792 | tf_op jit(solution)/shard_map/all_gather | solution.py:25
  653.0 250.2 %all-gather.13.cloned.1.call-start = ((), (), s32[]{:S(2)}) async-start(), calls=%async_computation.7 | async-start | bytes 9437184 | tf_op jit(solution)/shard_map/all_gather | solution.py:31
  824.5 453.1 %reduce-scatter.5.cloned.1.call-start = ((), (), s32[]{:S(2)}) async-start(), calls=%async_computation.5 | async-start | bytes 35651584 | tf_op jit(solution)/shard_map/reduce_scatter | solution.py:42
  908.6 2.8 copy-start.1
  1277.6 3.0 copy-start.3
Sparse Core Ops, SparseCore 0:
  10.8 129.6 all-gather.6
  184.5 78.5 all-gather.10
  310.8 332.7 reduce-scatter.2
  653.1 125.9 all-gather.8
  824.6 78.5 all-gather.12
  944.8 332.7 reduce-scatter.4
